TPU v7x, 128 devices: a whole 4x4x4 slice. The times are simulated.
128 devices in a mesh: dp: 16 (over z, x), tensor: 8 (over y, core).
Axes of the slice: x: 4, y: 4, z: 4, core: 2. Of those that a mesh axis runs over, the one named last changes fastest.
Arguments:
- acts: bfloat16 [49152, 8192], P('dp', 'tensor'), may hold values from -60 to 60
- cotangent: bfloat16 [49152, 2048], P(('dp', 'tensor')), may hold values from -6 to 6
- master: float32 [8192, 2048], P('tensor', 'dp'), may hold values from -0.0625 to 0.0625
- first_moment: float32 [8192, 2048], P('tensor', 'dp'), may hold values from -4 to 4
- second_moment: float32 [8192, 2048], P('tensor', 'dp'), may hold values from 0.01 to 1
Outputs:
- new_master: float32 [8192, 2048], P('tensor', 'dp')
- new_first: float32 [8192, 2048], P('tensor', 'dp')
- new_second: float32 [8192, 2048], P('tensor', 'dp')
- weights: bfloat16 [8192, 2048], P('tensor')
- block_scales: float32 [64, 16], P('tensor')
All inputs are finite; a program needn't handle non-finite values.
Results may differ from a plain program's by a relative error of at most 0.02.
Values may be sent and summed in bfloat16 or wider, within the bound.
A program may use at most 192 MiB of HBM per device.

v0:
```python
import math

import jax
import jax.numpy as jnp
from jax import lax
from jax.sharding import PartitionSpec as P

BLOCK = 128


def contract_rows(left, right):
    return lax.dot_general(
        left, right, (((0,), (0,)), ((), ())), preferred_element_type=jnp.float32
    )


def body(acts, cotangent, master, first_moment, second_moment):
    width_rows = acts.shape[1]
    columns = cotangent.shape[1]
    whole = lax.all_gather(cotangent, "tensor", axis=0, tiled=True)
    partial_value = contract_rows(acts, whole)
    magnitude = jnp.abs(partial_value).reshape(width_rows // BLOCK, BLOCK, columns // BLOCK, BLOCK)
    local_max = jnp.max(magnitude, axis=(1, 3))
    block_scales = lax.pmax(local_max, "dp") + 1e-06
    wide_scale = jnp.repeat(jnp.repeat(block_scales, BLOCK, axis=0), BLOCK, axis=1)
    quantized = (partial_value / wide_scale).astype(jnp.bfloat16)
    quantized = lax.optimization_barrier(quantized)
    summed = lax.psum_scatter(
        quantized.astype(jnp.float32).astype(jnp.bfloat16), "dp", scatter_dimension=1, tiled=True
    ).astype(jnp.float32)
    owned_width = summed.shape[1]
    owner = lax.axis_index("dp")
    own_scale = lax.dynamic_slice_in_dim(wide_scale, owner * owned_width, owned_width, 1)
    token_count = acts.shape[0] * lax.axis_size("dp")
    gradient = summed * own_scale / math.sqrt(token_count)
    new_first = 0.9 * first_moment + 0.1 * gradient
    new_second = 0.95 * second_moment + 0.05 * gradient * gradient
    first_hat = new_first / (1.0 - 0.9**10)
    second_hat = new_second / (1.0 - 0.95**10)
    new_master = master * (1.0 - 0.01 * 0.1) - 0.01 * first_hat / (jnp.sqrt(second_hat) + 1e-08)
    owned_weights = new_master.astype(jnp.bfloat16)
    weights = lax.all_gather(owned_weights, "dp", axis=1, tiled=True)
    return (new_master, new_first, new_second, weights, block_scales)


def solution(mesh):
    in_specs = (
        P("dp", "tensor"),
        P(("dp", "tensor"), None),
        P("tensor", "dp"),
        P("tensor", "dp"),
        P("tensor", "dp"),
    )
    out_specs = (
        P("tensor", "dp"),
        P("tensor", "dp"),
        P("tensor", "dp"),
        P("tensor", None),
        P("tensor", None),
    )
    return jax.shard_map(body, mesh=mesh, in_specs=in_specs, out_specs=out_specs, check_vma=False)
```

profile of v0, /device:TPU:0, one launch (start us, length us, event | category | flops | bytes accessed | tf_op | source)
XLA Modules:
  0.0 313.9 jit_solution(4201569831538639560)
XLA Ops:
  7.2 0.0 all-gather.3.cloned.1.call-start
  7.2 0.7 all-gather.3.cloned.1.call-update
  7.9 0.0 reduce-scatter.4.cloned.1.call-start
  7.9 71.6 %all-gather.3.cloned.1.call-done = bf16[3072,2048]{1,0:T(8,128)(2,1)} async-done(((bf16[384,2048]{1,0:T(8,128)(2,1)}), bf16[3072,2048]{1,0:T(8,128)(2,1)}) %all-gather.3.cloned.1.call-update) | async-done | bytes 12582928 | tf_op jit(solution)/shard_map/all_gather | solution.py:20
  79.5 17.4 %fusion.1 = f32[1024,2048]{1,0:T(8,128)S(1)} fusion(bf16[3072,1024]{1,0:T(8,128)(2,1)} %param.5, bf16[3072,2048]{1,0:T(8,128)(2,1)} %all-gather.3.cloned.1.call-done), kind=kOutput, calls=%fused_computation.10 | convolution fusion | flops 12884901888 | bytes 27262976 | tf_op jit(solution)/shard_map/dot_general | solution.py:12
  96.9 0.0 copy-start.1
  96.9 4.6 %abs_bitcast_fusion = f32[128,8,16,128]{3,1,2,0:T(8,128)} fusion(f32[1024,2048]{1,0:T(8,128)S(1)} %fusion.1), kind=kLoop, calls=%fused_computation.3 | loop fusion | flops 2097152 | bytes 16777216
  101.6 1.1 copy-done.1
  102.6 5.4 %copy.12 = f32[128,8,16,128]{3,2,1,0:T(8,128)S(1)} copy(f32[128,8,16,128]{3,1,2,0:T(8,128)} %abs_bitcast_fusion) | data formatting | bytes 16777216
  108.0 0.5 bitcast_reduce_fusion
  108.5 40.6 %pmax.7 = f32[8,16]{1,0:T(8,128)S(1)} all-reduce(f32[8,16]{1,0:T(8,128)S(1)} %bitcast_reduce_fusion), channel_id=1, replica_groups=mesh['dp'=16,'tensor'=8] {'dp'}, use_global_device_ids=true, to_apply=%region_1.0 | all-reduce | flops 128 | bytes 1024 | tf_op jit(solution)/shard_map/pmax | solution.py:24
  149.1 2.3 broadcast_in_dim.7
  151.5 0.0 copy-start
  151.5 3.2 %copy-done = f32[1024,16,128]{2,1,0:T(8,128)} copy-done((f32[1024,16,128]{2,1,0:T(8,128)}, f32[1024,16,128]{2,1,0:T(8,128)S(1)}, u32[]{:S(2)}) %copy-start) | copy-done | bytes 8388632
  154.7 7.4 %divide_convert_fusion = bf16[1024,2048]{1,0:T(8,128)(2,1)} fusion(f32[1024,2048]{1,0:T(8,128)} %copy-done.1, f32[128,8,16,128]{3,2,1,0:T(8,128)S(1)} %bitcast.17), kind=kLoop, calls=%fused_computation.2 | loop fusion | flops 4194304 | bytes 20971520 | tf_op jit(solution)/shard_map/convert_element_type | solution.py:26
  162.1 0.0 copy-done.5
  162.1 6.4 %copy.10 = bf16[1024,2048]{0,1:T(8,128)(2,1)} copy(bf16[1024,2048]{1,0:T(8,128)(2,1)} %divide_convert_fusion) | data formatting | bytes 8388608
  168.5 0.0 reduce-scatter.4.cloned.1.call-update
  168.5 0.2 all-gather.5.cloned.1.call-start
  168.8 0.0 copy-start.2
  168.8 0.0 copy-start.3
  168.8 0.0 copy-start.4
  168.8 10.8 %copy.17 = f32[128,8,16,128]{3,1,2,0:T(8,128)} copy(f32[128,8,16,128]{3,2,1,0:T(8,128)} %bitcast.18) | data formatting | bytes 16777216
  179.6 62.2 %reduce-scatter.4.cloned.1.call-done = bf16[128,1024]{1,0:T(8,128)(2,1)} async-done(((bf16[2048,1024]{1,0:T(8,128)(2,1)}), bf16[128,1024]{1,0:T(8,128)(2,1)}) %reduce-scatter.4.cloned.1.call-update) | async-done | bytes 262160
  241.8 1.1 copy.11
  243.0 0.0 copy-done.2
  243.0 0.0 copy-done.3
  243.0 0.0 copy-done.4
  243.0 2.5 fusion
  245.5 0.0 all-gather.5.cloned.1.call-update
  245.6 57.1 %all-gather.5.cloned.1.call-done = bf16[1024,2048]{1,0:T(8,128)(2,1)} async-done(((bf16[1024,128]{1,0:T(8,128)(2,1)}), bf16[1024,2048]{1,0:T(8,128)(2,1)}) %all-gather.5.cloned.1.call-update) | async-done | bytes 4194320 | tf_op jit(solution)/shard_map/all_gather | solution.py:42
  302.6 4.8 %copy.19 = bf16[1024,2048]{1,0:T(8,128)(2,1)} copy(bf16[1024,2048]{1,0:T(8,128)(2,1)} %all-gather.5.cloned.1.call-done) | data formatting | bytes 8388608
  (3 shorter events, 0.0 us)
Async XLA Ops:
  7.2 72.4 %all-gather.3.cloned.1.call-start = ((), (), s32[]{:S(2)}) async-start(), calls=%async_computation.1 | async-start | bytes 14155776 | tf_op jit(solution)/shard_map/all_gather | solution.py:20
  7.9 233.9 %reduce-scatter.4.cloned.1.call-start = ((), (), s32[]{:S(2)}) async-start(), calls=%async_computation.3 | async-start | bytes 4456448
  96.9 5.7 %copy-start.1 = (f32[1024,2048]{1,0:T(8,128)}, f32[1024,2048]{1,0:T(8,128)S(1)}, u32[]{:S(2)}) copy-start(f32[1024,2048]{1,0:T(8,128)S(1)} %fusion.1) | copy-start | bytes 25165828
  149.1 13.0 %copy-start.5 = (f32[8,16]{1,0:T(8,128)}, f32[8,16]{1,0:T(8,128)S(1)}, u32[]{:S(2)}) copy-start(f32[8,16]{1,0:T(8,128)S(1)} %broadcast_add_fusion) | copy-start | bytes 1540
  151.5 3.2 %copy-start = (f32[1024,16,128]{2,1,0:T(8,128)}, f32[1024,16,128]{2,1,0:T(8,128)S(1)}, u32[]{:S(2)}) copy-start(f32[1024,16,128]{2,1,0:T(8,128)S(1)} %broadcast_in_dim.7) | copy-start | bytes 25165828
  168.5 134.1 %all-gather.5.cloned.1.call-start = ((), (), s32[]{:S(2)}) async-start(), calls=%async_computation.2 | async-start | bytes 4456448 | tf_op jit(solution)/shard_map/all_gather | solution.py:42
  168.8 74.2 %copy-start.2 = (f32[1024,128]{1,0:T(8,128)S(1)}, f32[1024,128]{1,0:T(8,128)}, u32[]{:S(2)}) copy-start(f32[1024,128]{1,0:T(8,128)} %param.7) | copy-start | bytes 1572868
  168.8 74.2 %copy-start.3 = (f32[1024,128]{1,0:T(8,128)S(1)}, f32[1024,128]{1,0:T(8,128)}, u32[]{:S(2)}) copy-start(f32[1024,128]{1,0:T(8,128)} %param.8) | copy-start | bytes 1572868
  168.8 74.2 %copy-start.4 = (f32[1024,128]{1,0:T(8,128)S(1)}, f32[1024,128]{1,0:T(8,128)}, u32[]{:S(2)}) copy-start(f32[1024,128]{1,0:T(8,128)} %param.9) | copy-start | bytes 1572868
Sparse Core Ops, SparseCore 0:
  9.7 69.8 all-gather.2
  168.7 73.1 reduce-scatter.3
  245.7 56.8 all-gather.4
where the time goes:
time: 314 us
  waiting for transfers between devices  192 us (61%)
  blocking collectives  40.6 us (13%)
  local copies, waits for them, and re-layouts  35.2 us (11%)
  matrix products  17.4 us (6%)
  other arithmetic  15.1 us (5%)
  between operations  13.9 us (4%)
    all_gather x1, waiting for transfers between devices, body(): whole = lax.all_gather(cotangent, 'tensor', axis=0, tiled=True)  71.6 us
    unnamed x4, waiting for transfers between devices  62.9 us
    all_gather x1, waiting for transfers between devices, body(): weights = lax.all_gather(owned_weights, 'dp', axis=1, tiled=True)  57.1 us
    pmax x1, blocking collectives, body(): block_scales = lax.pmax(local_max, 'dp') + 1e-06  40.6 us
    unnamed x17, local copies, waits for them, and re-layouts  32.8 us
    dot_general x1, matrix products, contract_rows(): lax.dot_general(left, right, (((0,), (0,)), ((), ())), preferred_element_...  17.4 us
    convert_element_type x1, other arithmetic, body(): quantized = (partial_value / wide_scale).astype(jnp.bfloat16)  7.42 us
  transfers between devices with their start and end apart: 3, of which 3 were waited for; matrix products, arithmetic and copies ran while one was open for 3% of the time, Pallas kernels for 0%

commit v1 on v0

v1 whole, which is shorter than its diff:
```python
import functools
import math

import jax
import jax.numpy as jnp
from jax import lax
from jax.experimental import pallas as pl
from jax.experimental.pallas import tpu as pltpu
from jax.sharding import PartitionSpec as P

MESH = pl.DeviceIdType.MESH
BLOCK = 128
RING = 4
PAIRS = 8
F32 = jnp.float32
BF16 = jnp.bfloat16


def schedule():
    ops = [("own", 0), ("own", 1), ("turn",)]
    for s in range(PAIRS + 1):
        if s < PAIRS:
            ops += [("near", s)]
            if s + 2 < PAIRS:
                ops += [("own", s + 2)]
        if s >= 1:
            ops += [("far", s - 1)]
            d, odd = (s - 1) // 2, (s - 1) % 2
            if odd:
                if d >= 1:
                    ops += [("w1", d - 1, 0), ("w1", d - 1, 1)]
                ops += [("mm", s - 1, 0), ("r1a", d, 0), ("mm", s - 1, 1), ("r1a", d, 1)]
                if d >= 1:
                    ops += [("w2", d - 1, 0), ("w2", d - 1, 1)]
                ops += [("r1b", d, 0), ("r1b", d, 1)]
            else:
                ops += [("mm", s - 1, 0), ("mm", s - 1, 1)]
                if d >= 1:
                    ops += [("r1c", d - 1, 0), ("r1c", d - 1, 1), ("u", d - 1, 0), ("u", d - 1, 1)]
                if d >= 2:
                    ops += [("w3", d - 2, 0), ("w3", d - 2, 1)]
    last = RING - 1
    ops += [("mx0",)]
    for name in ("r1c", "u", "w1", "w2"):
        ops += [(name, last, 0), (name, last, 1)]
        if name == "r1c":
            ops += [("mx1",)]
        if name == "u":
            ops += [("mx2",)]
    for d in (last - 1, last):
        ops += [("w3", d, 0), ("w3", d, 1)]
    return ops


def kernel(
    token_count,
    acts, cotangent, master, first, second,
    new_master, new_first, new_second, weights, scales,
    plain, turned, cols, part, far_in, near_in, staged, sums_in, held,
    w_in, f_in, s_in, w_out, f_out, s_out,
    peak, peak_x, peak_z, peak_in,
    send, recv, local,
):
    dp, tensor = lax.axis_index("dp"), lax.axis_index("tensor")
    z, x = lax.div(dp, RING), lax.rem(dp, RING)
    y, core = lax.div(tensor, 2), lax.rem(tensor, 2)
    tokens, rows = plain.shape
    share = tokens // (2 * RING)
    half_rows = rows // 2
    quarter = half_rows // 2

    def at(dz=0, dx=0, dy=0, dc=0):
        return (
            lax.rem(z + dz, RING) * RING + lax.rem(x + dx, RING),
            lax.rem(y + dy, RING) * 2 + lax.rem(core + dc, 2),
        )

    counts = {"send": 0, "recv": 0, "local": 0}
    names = {}

    def sem(kind, *key, n=1):
        if (kind, key) not in names:
            names[kind, key] = counts[kind]
            counts[kind] += n
        return names[kind, key]

    drain = []

    def push(ref, key, device, dst=None, recv_at=None, when=None):
        at_recv = sem("recv", *key) if recv_at is None else recv_at
        copy = pltpu.make_async_remote_copy(
            src_ref=ref, dst_ref=ref if dst is None else dst,
            send_sem=send.at[sem("send", *key)], recv_sem=recv.at[at_recv],
            device_id=device, device_id_type=MESH,
        )
        copy.start()
        drain.append((ref, sem("send", *key), when))

    def arrived(ref, key, recv_at=None):
        at_recv = sem("recv", *key) if recv_at is None else recv_at
        pltpu.make_async_remote_copy(
            src_ref=ref, dst_ref=ref, send_sem=send.at[0], recv_sem=recv.at[at_recv],
            device_id=at(dc=1), device_id_type=MESH,
        ).wait_recv()

    def load(src, dst, *key):
        copy = pltpu.make_async_copy(src, dst, local.at[sem("local", *key)])
        copy.start()
        return copy

    def owner_of(d, j):
        return j * RING + (j + d) % RING

    mine = pl.ds(pl.multiple_of(tensor * share, share), share)
    own_loads = []
    for s in range(PAIRS):
        pair = []
        for h in range(2):
            column = owner_of(s // 2, s % 2 * 2 + h) * BLOCK
            pair.append(load(
                cotangent.at[:, pl.ds(column, BLOCK)],
                cols.at[s, mine, pl.ds(h * BLOCK, BLOCK)], "own", s, h,
            ))
        own_loads.append(pair)
    act_loads = [
        load(acts.at[pl.ds(i * share, share)], plain.at[pl.ds(i * share, share)], "acts", i)
        for i in range(2 * RING)
    ]
    state_loads = [
        load(a, b, "state", i) for i, (a, b) in enumerate(((master, w_in), (first, f_in), (second, s_in)))
    ]

    barrier = pltpu.get_barrier_semaphore()
    partners = [at(dy=1), at(dy=3), at(dc=1)]
    partners += [at(dx=i) for i in (1, 2, 3)] + [at(dz=i) for i in (1, 2, 3)]
    for device in partners:
        pl.semaphore_signal(barrier, inc=1, device_id=device, device_id_type=MESH)
    pl.semaphore_wait(barrier, len(partners))

    def token_rows(dy, dc=0, part_of=None):
        start = (lax.rem(y + dy, RING) * 2 + lax.rem(core + dc, 2)) * share
        size = share
        if part_of is not None:
            size = share // 2
            start = start + part_of * size
        return pl.ds(pl.multiple_of(start, size), size)

    def own(s):
        for copy in own_loads[s]:
            copy.wait()
        block = cols.at[s, token_rows(0)]
        push(block, ("g", s, "+"), at(dy=1))
        push(block, ("g", s, "-"), at(dy=3))
        push(block, ("g", s, "c", 0), at(dc=1))

    def near(s):
        for sign, dy, piece, to in (("+", 3, 0, 1), ("-", 1, 1, 3)):
            arrived(cols.at[s, token_rows(dy)], ("g", s, sign))
            push(cols.at[s, token_rows(dy, 0, piece)], ("gf", s, sign), at(dy=to))
            push(cols.at[s, token_rows(dy)], ("g", s, "c", dy), at(dc=1))

    def far(s):
        for sign, piece in (("+", 0), ("-", 1)):
            block = cols.at[s, token_rows(2, 0, piece)]
            arrived(block, ("gf", s, sign))
            push(block, ("gfc", s, sign), at(dc=1))
        for dy in (0, 1, 3):
            arrived(cols.at[s, token_rows(dy, 1)], ("g", s, "c", dy))
        for sign, piece in (("+", 0), ("-", 1)):
            arrived(cols.at[s, token_rows(2, 1, piece)], ("gfc", s, sign))

    def turn():
        for i, copy in enumerate(act_loads):
            copy.wait()
            for k in range(rows // 256):
                turned[pl.ds(k * 256, 256), pl.ds(i * share, share)] = (
                    plain[pl.ds(i * share, share), pl.ds(k * 256, 256)].T
                )
        peak[...] = jnp.zeros_like(peak)

    row_id = lax.broadcasted_iota(jnp.int32, peak.shape, 0)
    lane_id = lax.broadcasted_iota(jnp.int32, peak.shape, 1)

    def mm(s, t):
        d = s // 2

        def step(i, carry):
            start = pl.multiple_of(t * half_rows + i * 256, 256)
            value = jnp.dot(turned[pl.ds(start, 256), :], cols[s], preferred_element_type=F32)
            top = peak[...]
            for h in range(2):
                j = s % 2 * 2 + h
                block = value[:, h * BLOCK:(h + 1) * BLOCK]
                part[d, j, pl.ds(start, 256), :] = block.astype(BF16)
                for r in range(2):
                    largest = jnp.max(jnp.abs(block[r * BLOCK:(r + 1) * BLOCK]), axis=(0, 1), keepdims=True)
                    here = (row_id == t * (half_rows // BLOCK) + i * 2 + r) & (lane_id == owner_of(d, j))
                    top = jnp.where(here, largest, top)
            peak[...] = top
            return carry

        lax.fori_loop(0, half_rows // 256, step, 0)

    def first_axis(t, delta):
        return at(dx=delta) if t == 0 else at(dz=delta)

    def second_axis(t, delta):
        return at(dz=delta) if t == 0 else at(dx=delta)

    def target(d, t, delta):
        return lax.rem(x + delta - d + RING, RING) if t == 0 else lax.rem(z + delta, RING)

    def from_owner(d, t):
        return lax.rem(z - x + d + RING, RING) if t == 0 else lax.rem(x - z - d + 2 * RING, RING)

    def rows_of(t, piece=None):
        if piece is None:
            return pl.ds(t * half_rows, half_rows)
        return pl.ds(t * half_rows + piece * quarter, quarter)

    def r1a(d, t):
        distant = target(d, t, 2)
        for sign, piece, to in (("+", 0, 1), ("-", 1, 3)):
            push(part.at[d, distant, rows_of(t, piece)], ("r1f", d, t, sign), first_axis(t, to), dst=far_in.at[d, t, piece])
        for sign, piece, to in (("+", 0, 1), ("-", 1, 3)):
            push(
                part.at[d, target(d, t, to), rows_of(t, 1 - piece)], ("r1i", d, t, sign), first_axis(t, to),
                dst=near_in.at[d, t, piece, pl.ds((1 - piece) * quarter, quarter)],
            )

    def r1b(d, t):
        for sign, piece, to in (("+", 0, 1), ("-", 1, 3)):
            arrived(far_in.at[d, t, piece], ("r1f", d, t, sign))
            block = part.at[d, target(d, t, to), rows_of(t, piece)]
            block[...] = (block[...].astype(F32) + far_in[d, t, piece].astype(F32)).astype(BF16)
            push(
                block, ("r1d", d, t, sign), first_axis(t, to),
                dst=near_in.at[d, t, piece, pl.ds(piece * quarter, quarter)],
            )

    def r1c(d, t):
        for sign, piece in (("+", 0), ("-", 1)):
            arrived(near_in.at[d, t, piece, pl.ds((1 - piece) * quarter, quarter)], ("r1i", d, t, sign))
            arrived(near_in.at[d, t, piece, pl.ds(piece * quarter, quarter)], ("r1d", d, t, sign))
        total = part[d, target(d, t, 0), rows_of(t), :].astype(F32)
        total = total + near_in[d, t, 0].astype(F32) + near_in[d, t, 1].astype(F32)
        staged[d, t] = total.astype(BF16)
        delta = from_owner(d, t)
        away = delta != 0
        block = staged.at[d, t]
        base = sem("recv", "r2", t, n=3)

        @pl.when(away)
        def _():
            push(
                block, ("r2", d, t), second_axis(t, RING - delta),
                dst=sums_in.at[t, delta - 1], recv_at=base + delta - 1, when=away,
            )

    def owned(t, owner):
        return held.at[rows_of(t), pl.ds(pl.multiple_of(owner * BLOCK, BLOCK), BLOCK)]

    def u(d, t):
        delta = from_owner(d, t)
        base = sem("recv", "r2", t, n=3)
        block = owned(t, dp)
        at_owner = delta == 0

        @pl.when(at_owner)
        def _():
            if t == 0:
                for copy in state_loads:
                    copy.wait()
            total = staged[d, t].astype(F32)
            for i in range(3):
                arrived(sums_in.at[t, i], None, recv_at=base + i)
                total = total + sums_in[t, i].astype(F32)
            here = rows_of(t)
            gradient = total * (1.0 / math.sqrt(token_count))
            f_new = 0.9 * f_in[here, :] + 0.1 * gradient
            s_new = 0.95 * s_in[here, :] + 0.05 * gradient * gradient
            f_hat = f_new / (1.0 - 0.9**10)
            s_hat = s_new / (1.0 - 0.95**10)
            w_new = w_in[here, :] * (1.0 - 0.01 * 0.1) - 0.01 * f_hat / (jnp.sqrt(s_hat) + 1e-08)
            f_out[here, :] = f_new
            s_out[here, :] = s_new
            w_out[here, :] = w_new
            block[...] = w_new.astype(BF16)
            for i in (1, 2, 3):
                push(block, ("w1", d, t, i), second_axis(t, i), recv_at=sem("recv", "w1", d, t), when=at_owner)

    def block_at(d, t, delta):
        if t == 0:
            ox = lax.rem(x + delta, RING)
            oz = lax.rem(ox - d + RING, RING)
        else:
            oz = lax.rem(z + delta, RING)
            ox = lax.rem(oz + d, RING)
        return oz * RING + ox

    def w1(d, t):
        block = owned(t, block_at(d, t, 0))

        @pl.when(from_owner(d, t) != 0)
        def _():
            arrived(block, None, recv_at=sem("recv", "w1", d, t))

        for sign, to in (("+", 1), ("-", 3)):
            push(block, ("w2", d, t, sign), first_axis(t, to))

    def half_block(d, t, delta, piece):
        owner = block_at(d, t, delta)
        return held.at[rows_of(t, piece), pl.ds(pl.multiple_of(owner * BLOCK, BLOCK), BLOCK)]

    def w2(d, t):
        for sign, piece, frm, to in (("+", 0, 3, 1), ("-", 1, 1, 3)):
            arrived(owned(t, block_at(d, t, frm)), ("w2", d, t, sign))
            push(half_block(d, t, frm, piece), ("w2f", d, t, sign), first_axis(t, to))

    out_copies = []

    def w3(d, t):
        for sign, piece in (("+", 0), ("-", 1)):
            arrived(half_block(d, t, 2, piece), ("w2f", d, t, sign))
        for j in range(RING):
            place = (rows_of(t), pl.ds(owner_of(d, j) * BLOCK, BLOCK))
            out_copies.append(load(held.at[place], weights.at[place], "out", d, t, j))

    def mx0():
        peak_x[...] = peak[...]
        for i in (1, 2, 3):
            push(peak_x, ("mx", i), at(dx=i), dst=peak_in.at[i - 1])

    def mx1():
        top = peak_x[...]
        for i in (1, 2, 3):
            arrived(peak_in.at[i - 1], ("mx", i))
            top = jnp.maximum(top, peak_in[i - 1])
        peak_z[...] = top
        for i in (1, 2, 3):
            push(peak_z, ("mz", i), at(dz=i), dst=peak_in.at[i + 2])

    def mx2():
        top = peak_z[...]
        for i in (1, 2, 3):
            arrived(peak_in.at[i + 2], ("mz", i))
            top = jnp.maximum(top, peak_in[i + 2])
        scales[...] = top[:, : scales.shape[1]] + 1e-06

    steps = {f.__name__: f for f in (own, near, far, turn, mm, r1a, r1b, r1c, u, w1, w2, w3, mx0, mx1, mx2)}
    for name, *args in schedule():
        steps[name](*args)

    for i, (a, b) in enumerate(((w_out, new_master), (f_out, new_first), (s_out, new_second))):
        out_copies.append(load(a, b, "state out", i))

    def sent(ref, index):
        pltpu.make_async_remote_copy(
            src_ref=ref, dst_ref=ref, send_sem=send.at[index], recv_sem=recv.at[0],
            device_id=at(dc=1), device_id_type=MESH,
        ).wait_send()

    for ref, index, when in drain:
        if when is None:
            sent(ref, index)
        else:
            pl.when(when)(functools.partial(sent, ref, index))
    for copy in out_copies:
        copy.wait()


def body(acts, cotangent, master, first_moment, second_moment):
    tokens, rows = acts.shape
    columns = cotangent.shape[1]
    half = rows // 2
    state = jax.ShapeDtypeStruct(master.shape, F32)
    anywhere = pl.BlockSpec(memory_space=pl.ANY)
    vmem = pltpu.VMEM
    scratch = [
        vmem((tokens, rows), BF16),
        vmem((rows, tokens), BF16),
        vmem((PAIRS, tokens, 2 * BLOCK), BF16),
        vmem((RING, RING, rows, BLOCK), BF16),
        vmem((RING, 2, 2, half // 2, BLOCK), BF16),
        vmem((RING, 2, 2, half, BLOCK), BF16),
        vmem((RING, 2, half, BLOCK), BF16),
        vmem((2, 3, half, BLOCK), BF16),
        vmem((rows, columns), BF16),
    ]
    scratch += [vmem(master.shape, F32)] * 6
    scratch += [vmem((8, BLOCK), F32)] * 3 + [vmem((6, 8, BLOCK), F32)]
    scratch += [
        pltpu.SemaphoreType.DMA((200,)),
        pltpu.SemaphoreType.DMA((200,)),
        pltpu.SemaphoreType.DMA((64,)),
    ]
    return pl.pallas_call(
        functools.partial(kernel, tokens * lax.axis_size("dp")),
        out_shape=[
            state, state, state,
            jax.ShapeDtypeStruct((rows, columns), BF16),
            jax.ShapeDtypeStruct((rows // BLOCK, columns // BLOCK), F32),
        ],
        in_specs=[anywhere] * 5,
        out_specs=[anywhere] * 4 + [pl.BlockSpec(memory_space=pltpu.VMEM)],
        scratch_shapes=scratch,
        compiler_params=pltpu.CompilerParams(
            collective_id=0, has_side_effects=True, vmem_limit_bytes=62 * 2**20
        ),
    )(acts, cotangent, master, first_moment, second_moment)


def solution(mesh):
    in_specs = (
        P("dp", "tensor"),
        P(("dp", "tensor"), None),
        P("tensor", "dp"),
        P("tensor", "dp"),
        P("tensor", "dp"),
    )
    out_specs = (
        P("tensor", "dp"),
        P("tensor", "dp"),
        P("tensor", "dp"),
        P("tensor", None),
        P("tensor", None),
    )
    return jax.shard_map(body, mesh=mesh, in_specs=in_specs, out_specs=out_specs, check_vma=False)
```

time: 314 us -> 161 us (0.51)
  waiting for transfers between devices: 192 us -> 0 us
  Pallas kernels: 0 us -> 149 us
  blocking collectives: 40.6 us -> 0 us
  local copies, waits for them, and re-layouts: 35.2 us -> 11 us
  matrix products: 17.4 us -> 0 us
  other arithmetic: 15.1 us -> 0 us
  between operations: 13.9 us -> 0.64 us
    pallas_call x0 -> x1, Pallas kernels: none -> 149 us  [body(): pl.pallas_call(functools.partial(kernel, tokens * lax.axis_size('dp')), o...]
    all_gather x2 -> x0, waiting for transfers between devices: 129 us -> none  [the longest x1 71.6 us: body(): whole = lax.all_gather(cotangent, 'tensor', axis=0, tiled=True)]
    unnamed x4 -> x0, waiting for transfers between devices: 62.9 us -> none
    pmax x1 -> x0, blocking collectives: 40.6 us -> none  [body(): block_scales = lax.pmax(local_max, 'dp') + 1e-06]
    unnamed x17 -> x7, local copies, waits for them, and re-layouts: 32.8 us -> 11 us
    dot_general x1 -> x0, matrix products: 17.4 us -> none  [contract_rows(): lax.dot_general(left, right, (((0,), (0,)), ((), ())), preferred_element_...]
    convert_element_type x2 -> x0, other arithmetic: 9.97 us -> none  [the longest x1 7.42 us: body(): quantized = (partial_value / wide_scale).astype(jnp.bfloat16)]
    unnamed x1 -> x0, other arithmetic: 4.63 us -> none
  transfers between devices with their start and end apart: 3 -> 0, of which waited for: 3 -> 0; matrix products, arithmetic and copies ran while one was open for 3% -> 0% of each run, Pallas kernels for 0% -> 0%
where the time goes in v1:
time: 161 us
  Pallas kernels  149 us (93%)
  local copies, waits for them, and re-layouts  11 us (7%)
    pallas_call x1, Pallas kernels, body(): pl.pallas_call(functools.partial(kernel, tokens * lax.axis_size('dp')), o...  149 us
    unnamed x7, local copies, waits for them, and re-layouts  11 us

profile of v1, /device:TPU:0, one launch (start us, length us, event | category | flops | bytes accessed | tf_op | source)
XLA Modules:
  0.0 160.8 jit_solution(3216323785805841763)
XLA Ops:
  0.6 149.2 %shard_map.92 = (f32[1024,128]{1,0:T(8,128)}, f32[1024,128]{1,0:T(8,128)}, f32[1024,128]{1,0:T(8,128)}, bf16[1024,2048]{1,0:T(8,128)(2,1)}, f32[8,16]{1,0:T(8,128)}) custom-call(bf16[3072,1024]{1,0:T(8,128)(2,1)} %acts.1, bf16[384,2048]{1,0:T(8,128)(2,1)} %cotangent.1, f32[1024,128]{1,0:T(8,128)} %master.1, f32[1024,128]{1,0:T(8,128)} %first.1, ...), custom_call_target="tpu_custom_call" | custom-call | tf_op jit(solution)/shard_map/pallas_call | solution.py:397
  149.9 1.9 %copy.15 = f32[1024,128]{1,0:T(8,128)} copy(f32[1024,128]{1,0:T(8,128)} %get-tuple-element.10) | data formatting | bytes 1048576
  151.7 1.9 %copy.16 = f32[1024,128]{1,0:T(8,128)} copy(f32[1024,128]{1,0:T(8,128)} %get-tuple-element.11) | data formatting | bytes 1048576
  153.6 1.9 %copy.17 = f32[1024,128]{1,0:T(8,128)} copy(f32[1024,128]{1,0:T(8,128)} %get-tuple-element.12) | data formatting | bytes 1048576
  155.5 0.0 copy-start
  155.5 4.8 %copy.18 = bf16[1024,2048]{1,0:T(8,128)(2,1)} copy(bf16[1024,2048]{1,0:T(8,128)(2,1)} %get-tuple-element.13) | data formatting | bytes 8388608
  160.2 0.0 copy-done
  160.2 0.6 copy.19
Async XLA Ops:
  155.5 4.8 %copy-start = (f32[8,16]{1,0:T(8,128)S(1)}, f32[8,16]{1,0:T(8,128)}, u32[]{:S(2)}) copy-start(f32[8,16]{1,0:T(8,128)} %get-tuple-element.14) | copy-start | bytes 1540

commit v2 on v0

v2 whole, which is shorter than its diff:
```python
import functools
import math

import jax
import jax.numpy as jnp
from jax import lax
from jax.experimental import pallas as pl
from jax.experimental.pallas import tpu as pltpu
from jax.sharding import PartitionSpec as P

MESH = pl.DeviceIdType.MESH
BLOCK = 128
RING = 4
PAIRS = 8
F32 = jnp.float32
BF16 = jnp.bfloat16


LAST = PAIRS - 1


def schedule():
    ops = [("own", 0), ("own", 1), ("hand",), ("turn",)]
    lag = {"r1c": 2, "u": 3, "w1": 4, "w2": 5}
    for i in range(PAIRS + 5):
        if i < PAIRS:
            ops.append(("near", i))
            if i + 2 < PAIRS:
                ops.append(("own", i + 2))
        s = i - 1
        if 0 <= s < PAIRS:
            ops.append(("far", s))
            for t in range(2):
                ops += [("mm", s, t), ("r1", s, t)]
        if s == LAST:
            ops.append(("mx0",))
        for name, back in lag.items():
            s = i - back
            if 0 <= s < PAIRS:
                ops += [(name, s, 0), (name, s, 1)]
                if s == LAST and name == "u":
                    ops.append(("mx1",))
                if s == LAST and name == "w1":
                    ops += [("mx2",), ("states",)]
    ops += [("w3", s, t) for s in range(PAIRS) for t in range(2)]
    return ops


def adamw(master, first, second, gradient):
    f_new = 0.9 * first + 0.1 * gradient
    s_new = 0.95 * second + 0.05 * gradient * gradient
    f_hat = f_new / (1.0 - 0.9**10)
    s_hat = s_new / (1.0 - 0.95**10)
    w_new = master * (1.0 - 0.01 * 0.1) - 0.01 * f_hat / (jnp.sqrt(s_hat) + 1e-08)
    return w_new, f_new, s_new


def kernel(
    token_count,
    acts, cotangent, master, first, second,
    w_out, f_out, s_out, held, scales,
    plain, turned, cols, part, r1_in, once, r2_in, grads, grad_in,
    w_in, f_in, s_in, narrow, narrow_in,
    peak, peak_x, peak_z, peak_in,
    send, recv, local,
):
    dp, tensor = lax.axis_index("dp"), lax.axis_index("tensor")
    z, x = lax.div(dp, RING), lax.rem(dp, RING)
    y, core = lax.div(tensor, 2), lax.rem(tensor, 2)
    tokens, rows = plain.shape
    share = tokens // (2 * RING)
    half = rows // 2
    quarter = half // RING
    piece = quarter // RING

    def at(dz=0, dx=0, dy=0, dc=0):
        return (
            lax.rem(z + dz, RING) * RING + lax.rem(x + dx, RING),
            lax.rem(y + dy, RING) * 2 + lax.rem(core + dc, 2),
        )

    counts = {"send": 0, "recv": 0, "local": 0}
    names = {}

    def sem(kind, *key):
        if (kind, key) not in names:
            names[kind, key] = counts[kind]
            counts[kind] += 1
        return names[kind, key]

    def push(ref, key, device, dst=None):
        pltpu.make_async_remote_copy(
            src_ref=ref, dst_ref=ref if dst is None else dst,
            send_sem=send.at[sem("send", key[0])], recv_sem=recv.at[sem("recv", *key)],
            device_id=device, device_id_type=MESH,
        ).start()

    def arrived(ref, *key):
        pltpu.make_async_remote_copy(
            src_ref=ref, dst_ref=ref, send_sem=send.at[0], recv_sem=recv.at[sem("recv", *key)],
            device_id=at(dc=1), device_id_type=MESH,
        ).wait_recv()

    def sent(ref, kind, times=1):
        for _ in range(times):
            pltpu.make_async_remote_copy(
                src_ref=ref, dst_ref=ref, send_sem=send.at[sem("send", kind)], recv_sem=recv.at[0],
                device_id=at(dc=1), device_id_type=MESH,
            ).wait_send()

    def load(src, dst, *key):
        copy = pltpu.make_async_copy(src, dst, local.at[sem("local", *key)])
        copy.start()
        return copy

    def owner_of(s, h):
        d, j = s // 2, s % 2 + 2 * h
        return j * RING + (j + d) % RING

    barrier = pltpu.get_barrier_semaphore()
    partners = [at(dy=1), at(dy=3), at(dc=1)]
    partners += [at(dz=i // RING, dx=i % RING) for i in range(1, RING * RING)]
    for device in partners:
        pl.semaphore_signal(barrier, inc=1, device_id=device, device_id_type=MESH)

    mine = pl.ds(pl.multiple_of(tensor * share, share), share)
    own_loads = [
        [
            load(
                cotangent.at[:, pl.ds(owner_of(s, h) * BLOCK, BLOCK)],
                cols.at[s, mine, pl.ds(h * BLOCK, BLOCK)], "own", s, h,
            )
            for h in range(2)
        ]
        for s in range(PAIRS)
    ]
    state_loads = [
        load(a, b, "state", i) for i, (a, b) in enumerate(((master, w_in), (first, f_in), (second, s_in)))
    ]
    act_loads = [
        load(acts.at[pl.ds(i * share, share)], plain.at[pl.ds(i * share, share)], "acts", i)
        for i in range(2 * RING)
    ]

    pl.semaphore_wait(barrier, len(partners))

    def token_rows(dy, part_of=None):
        start = (lax.rem(y + dy, RING) * 2 + core) * share
        size = share
        if part_of is not None:
            size = share // 2
            start = start + part_of * size
        return pl.ds(pl.multiple_of(start, size), size)

    def own(s):
        for copy in own_loads[s]:
            copy.wait()
        block = cols.at[s, token_rows(0)]
        push(block, ("g", s, "+"), at(dy=1))
        push(block, ("g", s, "-"), at(dy=3))
        push(block, ("g", s, "c"), at(dc=1))

    def near(s):
        for sign, dy, k, to in (("+", 3, 0, 1), ("-", 1, 1, 3)):
            arrived(cols.at[s, token_rows(dy)], "g", s, sign)
            push(cols.at[s, token_rows(dy, k)], ("gf", s), at(dy=to))
            push(cols.at[s, token_rows(dy)], ("g", s, "c"), at(dc=1))

    def far(s):
        block = cols.at[s, token_rows(2)]
        arrived(block, "gf", s)
        push(block, ("g", s, "c"), at(dc=1))
        arrived(cols.at[s, pl.ds(0, tokens // 2)], "g", s, "c")

    def turn():
        for i, copy in enumerate(act_loads):
            copy.wait()
            for k in range(rows // 256):
                turned[pl.ds(k * 256, 256), pl.ds(i * share, share)] = (
                    plain[pl.ds(i * share, share), pl.ds(k * 256, 256)].T
                )
        peak[...] = jnp.zeros_like(peak)

    row_id = lax.broadcasted_iota(jnp.int32, peak.shape, 0)
    lane_id = lax.broadcasted_iota(jnp.int32, peak.shape, 1)

    def mm(s, t):
        def step(i, carry):
            start = pl.multiple_of(t * half + i * 256, 256)
            value = jnp.dot(turned[pl.ds(start, 256), :], cols[s], preferred_element_type=F32)
            part[s, pl.ds(start, 256), :] = value.astype(BF16)
            top = peak[...]
            for h in range(2):
                for r in range(2):
                    block = value[r * BLOCK:(r + 1) * BLOCK, h * BLOCK:(h + 1) * BLOCK]
                    largest = jnp.max(jnp.abs(block), axis=(0, 1), keepdims=True)
                    here = (row_id == t * (half // BLOCK) + i * 2 + r) & (lane_id == owner_of(s, h))
                    top = jnp.where(here, largest, top)
            peak[...] = top
            return carry

        lax.fori_loop(0, half // 256, step, 0)

    def along(t, axis, delta):
        return at(dx=delta) if t == axis else at(dz=delta)

    def quarter_rows(t, delta=0):
        place = lax.rem((x if t == 0 else z) + delta, RING)
        return pl.ds(pl.multiple_of(t * half + place * quarter, quarter), quarter)

    def piece_of(t, delta=0):
        place = lax.rem((z if t == 0 else x) + delta, RING)
        return pl.ds(pl.multiple_of(place * piece, piece), piece)

    def piece_rows(t):
        a, b = (x, z) if t == 0 else (z, x)
        return pl.ds(pl.multiple_of(t * half + a * quarter + b * piece, piece), piece)

    def hand():
        for copy in state_loads:
            copy.wait()
        for i, ref in enumerate((w_in, f_in, s_in)):
            narrow[i] = ref[...].astype(BF16)
        for t in range(2):
            narrow_in[t, dp] = narrow[:, piece_rows(t), :]
            for delta in range(1, RING * RING):
                dz, dx = delta // RING, delta % RING
                a, b = lax.rem(x + dx, RING), lax.rem(z + dz, RING)
                if t == 1:
                    a, b = b, a
                here = pl.ds(pl.multiple_of(t * half + a * quarter + b * piece, piece), piece)
                push(narrow.at[:, here], ("hand",), at(dz=dz, dx=dx), dst=narrow_in.at[t, dp])

    def r1(s, t):
        for delta in (1, 3, 2):
            push(part.at[s, quarter_rows(t, delta)], ("r1", s, t), along(t, 0, delta), dst=r1_in.at[s, t, delta - 1])

    def r1c(s, t):
        arrived(r1_in.at[s, t], "r1", s, t)
        total = part[s, quarter_rows(t), :].astype(F32)
        for i in range(RING - 1):
            total = total + r1_in[s, t, i].astype(F32)
        once[s, t] = total.astype(BF16)
        for delta in (1, 3, 2):
            push(once.at[s, t, piece_of(t, delta)], ("r2", s, t), along(t, 1, delta), dst=r2_in.at[s, t, delta - 1])

    def u(s, t):
        if (s, t) == (0, 0):
            arrived(narrow_in.at[:, pl.ds(0, RING * RING - 1)], "hand")
        arrived(r2_in.at[s, t], "r2", s, t)
        total = once[s, t, piece_of(t), :].astype(F32)
        for i in range(RING - 1):
            total = total + r2_in[s, t, i].astype(F32)
        total = total.astype(BF16)
        for h in range(2):
            owner = owner_of(s, h)
            block = total[:, h * BLOCK:(h + 1) * BLOCK]
            grads[s, t, h] = block
            source = grads.at[s, t, h]
            place = grad_in.at[piece_rows(t)]

            @pl.when(dp != owner)
            def _():
                push(source, ("grad",), (owner, tensor), dst=place)

            @pl.when(dp == owner)
            def _():
                place[...] = source[...]

            state = [narrow_in[t, owner, i].astype(F32) for i in range(3)]
            gradient = block.astype(F32) * (1.0 / math.sqrt(token_count))
            held[s, piece_rows(t), h * BLOCK:(h + 1) * BLOCK] = adamw(*state, gradient)[0].astype(BF16)
        for delta in (1, 3, 2):
            push(held.at[s, piece_rows(t)], ("w1", s, t), along(t, 1, delta))

    def w1(s, t):
        arrived(held.at[s, pl.ds(0, 3 * piece)], "w1", s, t)
        for delta in (1, 3):
            push(held.at[s, quarter_rows(t)], ("w2", s, t), along(t, 0, delta))

    def w2(s, t):
        arrived(held.at[s, pl.ds(0, 2 * quarter)], "w2", s, t)
        for k, to in ((0, 1), (1, 3)):
            start = quarter_rows(t, RING - to).start + k * (quarter // 2)
            block = held.at[s, pl.ds(pl.multiple_of(start, quarter // 2), quarter // 2)]
            push(block, ("w2f", s, t), along(t, 0, to))

    def w3(s, t):
        arrived(held.at[s, pl.ds(0, quarter)], "w2f", s, t)

    def states():
        arrived(grad_in.at[pl.ds(0, rows - 2 * piece)], "grad")
        gradient = grad_in[...].astype(F32) * (1.0 / math.sqrt(token_count))
        w_out[...], f_out[...], s_out[...] = adamw(w_in[...], f_in[...], s_in[...], gradient)

    def mx0():
        peak_x[...] = peak[...]
        for i in (1, 2, 3):
            push(peak_x, ("mx",), at(dx=i), dst=peak_in.at[i - 1])

    def mx1():
        arrived(peak_in.at[pl.ds(0, 3)], "mx")
        top = jnp.maximum(jnp.maximum(peak_in[0], peak_in[1]), jnp.maximum(peak_in[2], peak_x[...]))
        peak_z[...] = top
        for i in (1, 2, 3):
            push(peak_z, ("mz",), at(dz=i), dst=peak_in.at[i + 2])

    def mx2():
        arrived(peak_in.at[pl.ds(3, 3)], "mz")
        top = jnp.maximum(jnp.maximum(peak_in[3], peak_in[4]), jnp.maximum(peak_in[5], peak_z[...]))
        scales[...] = top[:, : scales.shape[1]] + 1e-06

    steps = {f.__name__: f for f in (own, near, far, hand, turn, mm, r1, r1c, u, w1, w2, w3, states, mx0, mx1, mx2)}
    for name, *args in schedule():
        steps[name](*args)

    sent(cols.at[:, pl.ds(0, 6 * share)], "g")
    sent(cols.at[:, pl.ds(0, share)], "gf")
    sent(narrow_in.at[:, pl.ds(0, RING * RING - 1)], "hand")
    sent(r1_in, "r1")
    sent(r2_in, "r2")
    sent(grad_in.at[pl.ds(0, rows - 2 * piece)], "grad")
    sent(held.at[:, pl.ds(0, 6 * piece)], "w1")
    sent(held.at[:, pl.ds(0, 4 * quarter)], "w2")
    sent(held.at[:, pl.ds(0, 2 * quarter)], "w2f")
    sent(peak_in.at[pl.ds(0, 3)], "mx")
    sent(peak_in.at[pl.ds(3, 3)], "mz")


def flush(*refs):
    count = (len(refs) - 1) // 2
    ins, outs, sems = refs[:count], refs[count:-1], refs[-1]
    copies = []

    def move(src, dst):
        copies.append(pltpu.make_async_copy(src, dst, sems.at[len(copies)]))
        copies[-1].start()

    for s in range(PAIRS):
        for h in range(2):
            j = s % 2 + 2 * h
            owner = j * RING + (j + s // 2) % RING
            move(ins[3].at[s, :, pl.ds(h * BLOCK, BLOCK)], outs[3].at[:, pl.ds(owner * BLOCK, BLOCK)])
    for i in (0, 1, 2, 4):
        move(ins[i], outs[i])
    for copy in copies:
        copy.wait()


def body(acts, cotangent, master, first_moment, second_moment):
    tokens, rows = acts.shape
    columns = cotangent.shape[1]
    state = pltpu.VMEM(master.shape, F32)
    anywhere = pl.BlockSpec(memory_space=pl.ANY)
    vmem = pltpu.VMEM
    quarter = rows // 2 // RING
    piece = quarter // RING
    scratch = [
        vmem((tokens, rows), BF16),
        vmem((rows, tokens), BF16),
        vmem((PAIRS, tokens, 2 * BLOCK), BF16),
        vmem((PAIRS, rows, 2 * BLOCK), BF16),
        vmem((PAIRS, 2, RING - 1, quarter, 2 * BLOCK), BF16),
        vmem((PAIRS, 2, quarter, 2 * BLOCK), BF16),
        vmem((PAIRS, 2, RING - 1, piece, 2 * BLOCK), BF16),
        vmem((PAIRS, 2, 2, piece, BLOCK), BF16),
        vmem(master.shape, BF16),
    ]
    scratch += [vmem(master.shape, F32)] * 3
    scratch += [vmem((3,) + master.shape, BF16), vmem((2, RING * RING, 3, piece, BLOCK), BF16)]
    scratch += [vmem((8, BLOCK), F32)] * 3 + [vmem((6, 8, BLOCK), F32)]
    scratch += [
        pltpu.SemaphoreType.DMA((12,)),
        pltpu.SemaphoreType.DMA((128,)),
        pltpu.SemaphoreType.DMA((32,)),
    ]
    results = pl.pallas_call(
        functools.partial(kernel, tokens * lax.axis_size("dp")),
        out_shape=[
            state, state, state,
            vmem((PAIRS, rows, 2 * BLOCK), BF16),
            vmem((rows // BLOCK, columns // BLOCK), F32),
        ],
        in_specs=[anywhere] * 5,
        out_specs=[pl.BlockSpec(memory_space=pltpu.VMEM)] * 5,
        scratch_shapes=scratch,
        compiler_params=pltpu.CompilerParams(
            collective_id=0, has_side_effects=True, vmem_limit_bytes=50 * 2**20
        ),
    )(acts, cotangent, master, first_moment, second_moment)
    shapes = [a.shape for a in results]
    shapes[3] = (rows, columns)
    return pl.pallas_call(
        flush,
        out_shape=[jax.ShapeDtypeStruct(shape, a.dtype) for shape, a in zip(shapes, results)],
        in_specs=[anywhere] * len(results),
        out_specs=[anywhere] * len(results),
        scratch_shapes=[pltpu.SemaphoreType.DMA((2 * PAIRS + 4,))],
        compiler_params=pltpu.CompilerParams(vmem_limit_bytes=2**20),
    )(*results)


def solution(mesh):
    in_specs = (
        P("dp", "tensor"),
        P(("dp", "tensor"), None),
        P("tensor", "dp"),
        P("tensor", "dp"),
        P("tensor", "dp"),
    )
    out_specs = (
        P("tensor", "dp"),
        P("tensor", "dp"),
        P("tensor", "dp"),
        P("tensor", None),
        P("tensor", None),
    )
    return jax.shard_map(body, mesh=mesh, in_specs=in_specs, out_specs=out_specs, check_vma=False)
```

time: 314 us -> 100 us (0.32)
  waiting for transfers between devices: 192 us -> 0 us
  Pallas kernels: 0 us -> 99.7 us
  blocking collectives: 40.6 us -> 0 us
  local copies, waits for them, and re-layouts: 35.2 us -> 0 us
  matrix products: 17.4 us -> 0 us
  other arithmetic: 15.1 us -> 0 us
  between operations: 13.9 us -> 0.64 us
    all_gather x2 -> x0, waiting for transfers between devices: 129 us -> none  [the longest x1 71.6 us: body(): whole = lax.all_gather(cotangent, 'tensor', axis=0, tiled=True)]
    pallas_call x0 -> x2, Pallas kernels: none -> 99.7 us  [the longest x1 97.1 us: body(): pl.pallas_call(functools.partial(kernel, tokens * lax.axis_size('dp')), o...]
    unnamed x4 -> x0, waiting for transfers between devices: 62.9 us -> none
    pmax x1 -> x0, blocking collectives: 40.6 us -> none  [body(): block_scales = lax.pmax(local_max, 'dp') + 1e-06]
    unnamed x17 -> x0, local copies, waits for them, and re-layouts: 32.8 us -> none
    dot_general x1 -> x0, matrix products: 17.4 us -> none  [contract_rows(): lax.dot_general(left, right, (((0,), (0,)), ((), ())), preferred_element_...]
    convert_element_type x2 -> x0, other arithmetic: 9.97 us -> none  [the longest x1 7.42 us: body(): quantized = (partial_value / wide_scale).astype(jnp.bfloat16)]
    unnamed x1 -> x0, other arithmetic: 4.63 us -> none
  transfers between devices with their start and end apart: 3 -> 0, of which waited for: 3 -> 0; matrix products, arithmetic and copies ran while one was open for 3% -> 0% of each run, Pallas kernels for 0% -> 0%
where the time goes in v2:
time: 100 us
  Pallas kernels  99.7 us (100%)
    pallas_call x1, Pallas kernels, body(): pl.pallas_call(functools.partial(kernel, tokens * lax.axis_size('dp')), o...  97.1 us
    pallas_call x1, Pallas kernels, body(): pl.pallas_call(flush, out_shape=[jax.ShapeDtypeStruct(shape, a.dtype) for...  2.67 us

profile of v2, /device:TPU:0, one launch (start us, length us, event | category | flops | bytes accessed | tf_op | source)
XLA Modules:
  0.0 100.4 jit_solution(8551695620274794258)
XLA Ops:
  0.6 97.1 %shard_map.92 = (f32[1024,128]{1,0:T(8,128)S(1)}, f32[1024,128]{1,0:T(8,128)S(1)}, f32[1024,128]{1,0:T(8,128)S(1)}, bf16[8,1024,256]{2,1,0:T(8,128)(2,1)S(1)}, f32[8,16]{1,0:T(8,128)S(1)}) custom-call(bf16[3072,1024]{1,0:T(8,128)(2,1)} %acts.1, bf16[384,2048]{1,0:T(8,128)(2,1)} %cotangent.1, f32[1024,128]{1,0:T(8,128)} %master.1, f32[1024,128]{1,0:T(8,128)} %first.1, ...), custom_call_target="tpu_custom_call" | custom-call | tf_op jit(solution)/shard_map/pallas_call | solution.py:377
  97.7 2.7 %shard_map.93 = (f32[1024,128]{1,0:T(8,128)}, f32[1024,128]{1,0:T(8,128)}, f32[1024,128]{1,0:T(8,128)}, bf16[1024,2048]{1,0:T(8,128)(2,1)}, f32[8,16]{1,0:T(8,128)}) custom-call(f32[1024,128]{1,0:T(8,128)S(1)} %get-tuple-element.10.refs_0_, f32[1024,128]{1,0:T(8,128)S(1)} %get-tuple-element.11.refs_1_, f32[1024,128]{1,0:T(8,128)S(1)} %get-tuple-element.12.refs_2_, ...), custom_call_target="tpu_custom_call" | custom-call | tf_op jit(solution)/shard_map/pallas_call | solution.py:393

commit v3 on v2

--- a/solution.py
+++ b/solution.py
@@ -16,33 +16,36 @@
 BF16 = jnp.bfloat16
 
 
-LAST = PAIRS - 1
+CHUNKS = [(s, (0, 1)) for s in range(PAIRS)]
+LAST = len(CHUNKS) - 1
+DIRECT = LAST
 
 
 def schedule():
     ops = [("own", 0), ("own", 1), ("hand",), ("turn",)]
-    lag = {"r1c": 2, "u": 3, "w1": 4, "w2": 5}
-    for i in range(PAIRS + 5):
-        if i < PAIRS:
-            ops.append(("near", i))
-            if i + 2 < PAIRS:
-                ops.append(("own", i + 2))
-        s = i - 1
-        if 0 <= s < PAIRS:
-            ops.append(("far", s))
+
+    def both(name, c):
+        return [(name, c, 0), (name, c, 1)] if 0 <= c <= LAST else []
+
+    for i in range(LAST + 1):
+        ops.append(("near", i))
+        if i + 2 <= LAST:
+            ops.append(("own", i + 2))
+        if i >= 1:
+            ops.append(("far", i - 1))
             for t in range(2):
-                ops += [("mm", s, t), ("r1", s, t)]
-        if s == LAST:
-            ops.append(("mx0",))
-        for name, back in lag.items():
-            s = i - back
-            if 0 <= s < PAIRS:
-                ops += [(name, s, 0), (name, s, 1)]
-                if s == LAST and name == "u":
-                    ops.append(("mx1",))
-                if s == LAST and name == "w1":
-                    ops += [("mx2",), ("states",)]
-    ops += [("w3", s, t) for s in range(PAIRS) for t in range(2)]
+                ops += [("mm", i - 1, t), ("r1", i - 1, t)]
+        ops += both("r1c", i - 2) + both("u", i - 3) + both("w1", i - 4) + both("w2", i - 5)
+    ops += both("mm_near", LAST) + [("far", LAST)]
+    for t in range(2):
+        ops += [("mm_far", LAST, t), ("r1", LAST, t)]
+    ops += both("late", LAST) + [("mx0",)]
+    ops += both("r1c", LAST - 1) + both("u", LAST - 2) + both("w1", LAST - 3) + both("w2", LAST - 4)
+    ops += both("r1c", LAST) + [("mx1",)] + both("u", LAST - 1) + both("w1", LAST - 2) + both("w2", LAST - 3)
+    ops += both("u", LAST) + [("mx2",)] + both("w1", LAST - 1) + both("w2", LAST - 2)
+    ops += both("w1", LAST) + both("w2", LAST - 1) + [("states",)] + both("w2", LAST)
+    for c in range(LAST + 1):
+        ops += both("w3", c)
     return ops
 
 
@@ -59,7 +62,7 @@
     token_count,
     acts, cotangent, master, first, second,
     w_out, f_out, s_out, held, scales,
-    plain, turned, cols, part, r1_in, once, r2_in, grads, grad_in,
+    plain, turned, cols, early, part, r1_in, once, r2_in, grads, grad_in,
     w_in, f_in, s_in, narrow, narrow_in,
     peak, peak_x, peak_z, peak_in,
     send, recv, local,
@@ -152,25 +155,35 @@
             start = start + part_of * size
         return pl.ds(pl.multiple_of(start, size), size)
 
-    def own(s):
-        for copy in own_loads[s]:
-            copy.wait()
-        block = cols.at[s, token_rows(0)]
-        push(block, ("g", s, "+"), at(dy=1))
-        push(block, ("g", s, "-"), at(dy=3))
-        push(block, ("g", s, "c"), at(dc=1))
-
-    def near(s):
+    def lanes(c):
+        return pl.ds(CHUNKS[c][1][0] * BLOCK, len(CHUNKS[c][1]) * BLOCK)
+
+    def own(c):
+        s, halves = CHUNKS[c]
+        for h in halves:
+            own_loads[s][h].wait()
+        block = cols.at[s, token_rows(0), lanes(c)]
+        push(block, ("g", c, "+"), at(dy=1))
+        push(block, ("g", c, "-"), at(dy=3))
+        push(block, ("g", c, "c"), at(dc=1))
+
+    def near(c):
+        s = CHUNKS[c][0]
         for sign, dy, k, to in (("+", 3, 0, 1), ("-", 1, 1, 3)):
-            arrived(cols.at[s, token_rows(dy)], "g", s, sign)
-            push(cols.at[s, token_rows(dy, k)], ("gf", s), at(dy=to))
-            push(cols.at[s, token_rows(dy)], ("g", s, "c"), at(dc=1))
-
-    def far(s):
-        block = cols.at[s, token_rows(2)]
-        arrived(block, "gf", s)
-        push(block, ("g", s, "c"), at(dc=1))
-        arrived(cols.at[s, pl.ds(0, tokens // 2)], "g", s, "c")
+            arrived(cols.at[s, token_rows(dy), lanes(c)], "g", c, sign)
+            push(cols.at[s, token_rows(dy, k), lanes(c)], ("gf", c), at(dy=to))
+            push(cols.at[s, token_rows(dy), lanes(c)], ("g", c, "c"), at(dc=1))
+
+    def far(c):
+        s = CHUNKS[c][0]
+        block = cols.at[s, token_rows(2), lanes(c)]
+        arrived(block, "gf", c)
+        if c < LAST:
+            push(block, ("g", c, "c"), at(dc=1))
+            arrived(cols.at[s, pl.ds(0, tokens // 2), lanes(c)], "g", c, "c")
+        else:
+            push(block, ("g", c, "cf"), at(dc=1))
+            arrived(block, "g", c, "cf")
 
     def turn():
         for i, copy in enumerate(act_loads):
@@ -184,22 +197,61 @@
     row_id = lax.broadcasted_iota(jnp.int32, peak.shape, 0)
     lane_id = lax.broadcasted_iota(jnp.int32, peak.shape, 1)
 
-    def mm(s, t):
-        def step(i, carry):
-            start = pl.multiple_of(t * half + i * 256, 256)
-            value = jnp.dot(turned[pl.ds(start, 256), :], cols[s], preferred_element_type=F32)
-            part[s, pl.ds(start, 256), :] = value.astype(BF16)
-            top = peak[...]
-            for h in range(2):
-                for r in range(2):
-                    block = value[r * BLOCK:(r + 1) * BLOCK, h * BLOCK:(h + 1) * BLOCK]
-                    largest = jnp.max(jnp.abs(block), axis=(0, 1), keepdims=True)
-                    here = (row_id == t * (half // BLOCK) + i * 2 + r) & (lane_id == owner_of(s, h))
-                    top = jnp.where(here, largest, top)
-            peak[...] = top
+    def chip_tokens(dy):
+        return pl.ds(pl.multiple_of(lax.rem(y + dy, RING) * 2 * share, 2 * share), 2 * share)
+
+    def product(start, c, dy):
+        here = chip_tokens(dy)
+        return jnp.dot(
+            turned[pl.ds(start, 256), here], cols[CHUNKS[c][0], here, lanes(c)], preferred_element_type=F32
+        )
+
+    def largest(c, t, i, value):
+        s, halves = CHUNKS[c]
+        top = peak[...]
+        for k, h in enumerate(halves):
+            for r in range(2):
+                block = value[r * BLOCK:(r + 1) * BLOCK, k * BLOCK:(k + 1) * BLOCK]
+                here = (row_id == t * (half // BLOCK) + i * 2 + r) & (lane_id == owner_of(s, h))
+                top = jnp.where(here, jnp.max(jnp.abs(block), axis=(0, 1), keepdims=True), top)
+        peak[...] = top
+
+    def in_steps(t, step):
+        def at_step(i, carry):
+            step(i, pl.multiple_of(t * half + i * 256, 256))
             return carry
 
-        lax.fori_loop(0, half // 256, step, 0)
+        lax.fori_loop(0, half // 256, at_step, 0)
+
+    def mm(c, t):
+        s = CHUNKS[c][0]
+
+        def step(i, start):
+            value = jnp.dot(turned[pl.ds(start, 256), :], cols[s, :, lanes(c)], preferred_element_type=F32)
+            part[s, pl.ds(start, 256), lanes(c)] = value.astype(BF16)
+            largest(c, t, i, value)
+
+        in_steps(t, step)
+
+    def mm_near(c, t):
+        if t == 0:
+            arrived(cols.at[CHUNKS[c][0], pl.ds(0, 3 * share), lanes(c)], "g", c, "c")
+
+        def step(i, start):
+            early[pl.ds(start, 256), :] = product(start, c, 0) + product(start, c, 1) + product(start, c, 3)
+
+        in_steps(t, step)
+
+    def mm_far(c, t):
+        def step(i, start):
+            value = early[pl.ds(start, 256), :] + product(start, c, 2)
+            part[CHUNKS[c][0], pl.ds(start, 256), lanes(c)] = value.astype(BF16)
+            early[pl.ds(start, 256), :] = value
+
+        in_steps(t, step)
+
+    def late(c, t):
+        in_steps(t, lambda i, start: largest(c, t, i, early[pl.ds(start, 256), :]))
 
     def along(t, axis, delta):
         return at(dx=delta) if t == axis else at(dz=delta)
@@ -231,62 +283,76 @@
                 here = pl.ds(pl.multiple_of(t * half + a * quarter + b * piece, piece), piece)
                 push(narrow.at[:, here], ("hand",), at(dz=dz, dx=dx), dst=narrow_in.at[t, dp])
 
-    def r1(s, t):
+    def r1(c, t):
+        s = CHUNKS[c][0]
         for delta in (1, 3, 2):
-            push(part.at[s, quarter_rows(t, delta)], ("r1", s, t), along(t, 0, delta), dst=r1_in.at[s, t, delta - 1])
-
-    def r1c(s, t):
-        arrived(r1_in.at[s, t], "r1", s, t)
-        total = part[s, quarter_rows(t), :].astype(F32)
+            push(
+                part.at[s, quarter_rows(t, delta), lanes(c)], ("r1", c, t), along(t, 0, delta),
+                dst=r1_in.at[s, t, delta - 1, :, lanes(c)],
+            )
+
+    def r1c(c, t):
+        s = CHUNKS[c][0]
+        arrived(r1_in.at[s, t, :, :, lanes(c)], "r1", c, t)
+        total = part[s, quarter_rows(t), lanes(c)].astype(F32)
         for i in range(RING - 1):
-            total = total + r1_in[s, t, i].astype(F32)
-        once[s, t] = total.astype(BF16)
+            total = total + r1_in[s, t, i, :, lanes(c)].astype(F32)
+        once[s, t, :, lanes(c)] = total.astype(BF16)
         for delta in (1, 3, 2):
-            push(once.at[s, t, piece_of(t, delta)], ("r2", s, t), along(t, 1, delta), dst=r2_in.at[s, t, delta - 1])
-
-    def u(s, t):
-        if (s, t) == (0, 0):
+            push(
+                once.at[s, t, piece_of(t, delta), lanes(c)], ("r2", c, t), along(t, 1, delta),
+                dst=r2_in.at[s, t, delta - 1, :, lanes(c)],
+            )
+
+    def u(c, t):
+        s, halves = CHUNKS[c]
+        if (c, t) == (0, 0):
             arrived(narrow_in.at[:, pl.ds(0, RING * RING - 1)], "hand")
-        arrived(r2_in.at[s, t], "r2", s, t)
-        total = once[s, t, piece_of(t), :].astype(F32)
+        arrived(r2_in.at[s, t, :, :, lanes(c)], "r2", c, t)
+        total = once[s, t, piece_of(t), lanes(c)].astype(F32)
         for i in range(RING - 1):
-            total = total + r2_in[s, t, i].astype(F32)
+            total = total + r2_in[s, t, i, :, lanes(c)].astype(F32)
         total = total.astype(BF16)
-        for h in range(2):
+        for k, h in enumerate(halves):
             owner = owner_of(s, h)
-            block = total[:, h * BLOCK:(h + 1) * BLOCK]
+            block = total[:, k * BLOCK:(k + 1) * BLOCK]
             grads[s, t, h] = block
-            source = grads.at[s, t, h]
-            place = grad_in.at[piece_rows(t)]
-
-            @pl.when(dp != owner)
-            def _():
-                push(source, ("grad",), (owner, tensor), dst=place)
-
-            @pl.when(dp == owner)
-            def _():
-                place[...] = source[...]
-
             state = [narrow_in[t, owner, i].astype(F32) for i in range(3)]
             gradient = block.astype(F32) * (1.0 / math.sqrt(token_count))
             held[s, piece_rows(t), h * BLOCK:(h + 1) * BLOCK] = adamw(*state, gradient)[0].astype(BF16)
         for delta in (1, 3, 2):
-            push(held.at[s, piece_rows(t)], ("w1", s, t), along(t, 1, delta))
-
-    def w1(s, t):
-        arrived(held.at[s, pl.ds(0, 3 * piece)], "w1", s, t)
-        for delta in (1, 3):
-            push(held.at[s, quarter_rows(t)], ("w2", s, t), along(t, 0, delta))
-
-    def w2(s, t):
-        arrived(held.at[s, pl.ds(0, 2 * quarter)], "w2", s, t)
-        for k, to in ((0, 1), (1, 3)):
+            push(held.at[s, piece_rows(t), lanes(c)], ("w1", c, t), along(t, 1, delta))
+        for h in halves:
+            owner = owner_of(s, h)
+            source = grads.at[s, t, h]
+            place = grad_in.at[piece_rows(t)]
+
+            @pl.when(dp != owner)
+            def _():
+                push(source, ("grad",), (owner, tensor), dst=place)
+
+            @pl.when(dp == owner)
+            def _():
+                place[...] = source[...]
+
+    def w1(c, t):
+        s = CHUNKS[c][0]
+        arrived(held.at[s, pl.ds(0, 3 * piece), lanes(c)], "w1", c, t)
+        for delta in (1, 3) if c < DIRECT else (2, 1, 3):
+            push(
+                held.at[s, quarter_rows(t), lanes(c)], ("w2" if delta != 2 else "w2f", c, t), along(t, 0, delta)
+            )
+
+    def w2(c, t):
+        s = CHUNKS[c][0]
+        arrived(held.at[s, pl.ds(0, 2 * quarter), lanes(c)], "w2", c, t)
+        for k, to in ((0, 1), (1, 3)) if c < DIRECT else ():
             start = quarter_rows(t, RING - to).start + k * (quarter // 2)
-            block = held.at[s, pl.ds(pl.multiple_of(start, quarter // 2), quarter // 2)]
-            push(block, ("w2f", s, t), along(t, 0, to))
-
-    def w3(s, t):
-        arrived(held.at[s, pl.ds(0, quarter)], "w2f", s, t)
+            block = held.at[s, pl.ds(pl.multiple_of(start, quarter // 2), quarter // 2), lanes(c)]
+            push(block, ("w2f", c, t), along(t, 0, to))
+
+    def w3(c, t):
+        arrived(held.at[CHUNKS[c][0], pl.ds(0, quarter), lanes(c)], "w2f", c, t)
 
     def states():
         arrived(grad_in.at[pl.ds(0, rows - 2 * piece)], "grad")
@@ -310,7 +376,7 @@
         top = jnp.maximum(jnp.maximum(peak_in[3], peak_in[4]), jnp.maximum(peak_in[5], peak_z[...]))
         scales[...] = top[:, : scales.shape[1]] + 1e-06
 
-    steps = {f.__name__: f for f in (own, near, far, hand, turn, mm, r1, r1c, u, w1, w2, w3, states, mx0, mx1, mx2)}
+    steps = {f.__name__: f for f in (own, near, far, hand, turn, mm, mm_near, mm_far, late, r1, r1c, u, w1, w2, w3, states, mx0, mx1, mx2)}
     for name, *args in schedule():
         steps[name](*args)
 
@@ -359,6 +425,7 @@
         vmem((tokens, rows), BF16),
         vmem((rows, tokens), BF16),
         vmem((PAIRS, tokens, 2 * BLOCK), BF16),
+        vmem((rows, len(CHUNKS[LAST][1]) * BLOCK), F32),
         vmem((PAIRS, rows, 2 * BLOCK), BF16),
         vmem((PAIRS, 2, RING - 1, quarter, 2 * BLOCK), BF16),
         vmem((PAIRS, 2, quarter, 2 * BLOCK), BF16),

time: 100 us -> 98.4 us (0.984)
  Pallas kernels: 99.7 us -> 97.4 us
    pallas_call x1, Pallas kernels: 97.1 us -> 94.7 us  [body(): pl.pallas_call(functools.partial(kernel, tokens * lax.axis_size('dp')), o...]
where the time goes in v3:
time: 98.4 us; the launch traced here: 98 us
  Pallas kernels  97.4 us (99%)
    pallas_call x1, Pallas kernels, body(): pl.pallas_call(functools.partial(kernel, tokens * lax.axis_size('dp')), o...  94.7 us
    pallas_call x1, Pallas kernels, body(): pl.pallas_call(flush, out_shape=[jax.ShapeDtypeStruct(shape, a.dtype) for...  2.67 us

profile of v3, /device:TPU:0, one launch (start us, length us, event | category | flops | bytes accessed | tf_op | source)
XLA Modules:
  0.0 98.0 jit_solution(2979272248948532427)
XLA Ops:
  0.6 94.7 %shard_map.92 = (f32[1024,128]{1,0:T(8,128)S(1)}, f32[1024,128]{1,0:T(8,128)S(1)}, f32[1024,128]{1,0:T(8,128)S(1)}, bf16[8,1024,256]{2,1,0:T(8,128)(2,1)S(1)}, f32[8,16]{1,0:T(8,128)S(1)}) custom-call(bf16[3072,1024]{1,0:T(8,128)(2,1)} %acts.1, bf16[384,2048]{1,0:T(8,128)(2,1)} %cotangent.1, f32[1024,128]{1,0:T(8,128)} %master.1, f32[1024,128]{1,0:T(8,128)} %first.1, ...), custom_call_target="tpu_custom_call" | custom-call | tf_op jit(solution)/shard_map/pallas_call | solution.py:444
  95.3 2.7 %shard_map.93 = (f32[1024,128]{1,0:T(8,128)}, f32[1024,128]{1,0:T(8,128)}, f32[1024,128]{1,0:T(8,128)}, bf16[1024,2048]{1,0:T(8,128)(2,1)}, f32[8,16]{1,0:T(8,128)}) custom-call(f32[1024,128]{1,0:T(8,128)S(1)} %get-tuple-element.10.refs_0_, f32[1024,128]{1,0:T(8,128)S(1)} %get-tuple-element.11.refs_1_, f32[1024,128]{1,0:T(8,128)S(1)} %get-tuple-element.12.refs_2_, ...), custom_call_target="tpu_custom_call" | custom-call | tf_op jit(solution)/shard_map/pallas_call | solution.py:460

commit v4 on v3

--- a/solution.py
+++ b/solution.py
@@ -398,17 +398,21 @@
     ins, outs, sems = refs[:count], refs[count:-1], refs[-1]
     copies = []
 
-    def move(src, dst):
-        copies.append(pltpu.make_async_copy(src, dst, sems.at[len(copies)]))
-        copies[-1].start()
+    def move(src, dst, cuts=1):
+        size = dst.shape[0] // cuts
+        for i in range(cuts):
+            here = pl.ds(i * size, size)
+            copies.append(pltpu.make_async_copy(src.at[here], dst.at[here], sems.at[len(copies)]))
+            copies[-1].start()
 
     for s in range(PAIRS):
         for h in range(2):
             j = s % 2 + 2 * h
             owner = j * RING + (j + s // 2) % RING
-            move(ins[3].at[s, :, pl.ds(h * BLOCK, BLOCK)], outs[3].at[:, pl.ds(owner * BLOCK, BLOCK)])
-    for i in (0, 1, 2, 4):
-        move(ins[i], outs[i])
+            move(ins[3].at[s, :, pl.ds(h * BLOCK, BLOCK)], outs[3].at[:, pl.ds(owner * BLOCK, BLOCK)], 2)
+    for i in (0, 1, 2):
+        move(ins[i], outs[i], 4)
+    move(ins[4], outs[4])
     for copy in copies:
         copy.wait()
 
@@ -462,7 +466,7 @@
         out_shape=[jax.ShapeDtypeStruct(shape, a.dtype) for shape, a in zip(shapes, results)],
         in_specs=[anywhere] * len(results),
         out_specs=[anywhere] * len(results),
-        scratch_shapes=[pltpu.SemaphoreType.DMA((2 * PAIRS + 4,))],
+        scratch_shapes=[pltpu.SemaphoreType.DMA((4 * PAIRS + 13,))],
         compiler_params=pltpu.CompilerParams(vmem_limit_bytes=2**20),
     )(*results)
 

time: 98.4 us -> 98.6 us (level)
  no operation moved by 1% of the time
where the time goes in v4:
time: 98.6 us; the launch traced here: 98.2 us
  Pallas kernels  97.6 us (99%)
    pallas_call x1, Pallas kernels, body(): pl.pallas_call(functools.partial(kernel, tokens * lax.axis_size('dp')), o...  94.7 us
    pallas_call x1, Pallas kernels, body(): pl.pallas_call(flush, out_shape=[jax.ShapeDtypeStruct(shape, a.dtype) for...  2.86 us

profile of v4, /device:TPU:0, one launch (start us, length us, event | category | flops | bytes accessed | tf_op | source)
XLA Modules:
  0.0 98.2 jit_solution(12808200007415369118)
XLA Ops:
  0.6 94.7 %shard_map.92 = (f32[1024,128]{1,0:T(8,128)S(1)}, f32[1024,128]{1,0:T(8,128)S(1)}, f32[1024,128]{1,0:T(8,128)S(1)}, bf16[8,1024,256]{2,1,0:T(8,128)(2,1)S(1)}, f32[8,16]{1,0:T(8,128)S(1)}) custom-call(bf16[3072,1024]{1,0:T(8,128)(2,1)} %acts.1, bf16[384,2048]{1,0:T(8,128)(2,1)} %cotangent.1, f32[1024,128]{1,0:T(8,128)} %master.1, f32[1024,128]{1,0:T(8,128)} %first.1, ...), custom_call_target="tpu_custom_call" | custom-call | tf_op jit(solution)/shard_map/pallas_call | solution.py:448
  95.3 2.9 %shard_map.93 = (f32[1024,128]{1,0:T(8,128)}, f32[1024,128]{1,0:T(8,128)}, f32[1024,128]{1,0:T(8,128)}, bf16[1024,2048]{1,0:T(8,128)(2,1)}, f32[8,16]{1,0:T(8,128)}) custom-call(f32[1024,128]{1,0:T(8,128)S(1)} %get-tuple-element.10.refs_0_, f32[1024,128]{1,0:T(8,128)S(1)} %get-tuple-element.11.refs_1_, f32[1024,128]{1,0:T(8,128)S(1)} %get-tuple-element.12.refs_2_, ...), custom_call_target="tpu_custom_call" | custom-call | tf_op jit(solution)/shard_map/pallas_call | solution.py:464
